TPU v7x, 32 devices: a whole 2x2x4 slice. The times are simulated.
32 devices in a mesh: blk: 8 (over z, x), mp: 4 (over y, core).
Axes of the slice: x: 2, y: 2, z: 4, core: 2. Of those that a mesh axis runs over, the one named last changes fastest.
Arguments:
- tokens_in: bfloat16 [2048, 2048], P('blk'), may hold values from -17 to 17
- w_qkv: bfloat16 [3, 2048, 2048], P(None, None, 'mp'), may hold values from -0.125 to 0.125
- w_out: bfloat16 [2048, 2048], P('mp'), may hold values from -0.125 to 0.125
- grad_y: bfloat16 [2048, 2048], P('blk'), may hold values from -6 to 6
- block_cols: int32 [16, 2], replicated, may hold values from 0 to 15, as said below
- block_count: int32 [16], replicated, may hold values from 1 to 2, as said below
Outputs:
- grad_x: bfloat16 [2048, 2048], P('blk', 'mp')
- grad_qkv: bfloat16 [3, 2048, 2048], P(None, 'blk', 'mp')
- grad_out: bfloat16 [2048, 2048], P('mp', 'blk')
Inputs may be any that keep to these rules, and one draw needn't show every extreme that they name: `block_cols`: slot 0 of row r is r itself; the first block_count[r] slots of a row are distinct blocks; later slots repeat r. `block_count`: some rows use all 2 slots.
All inputs are finite; a program needn't handle non-finite values.
Results may differ from a plain program's by a relative error of at most 0.02.
Values may be sent and summed in bfloat16 or wider, within the bound.
No kernel may reach another device: no remote copies, remote signals or barrier semaphores. Data moves between devices by JAX's collectives and lax.ppermute only.
A program may use at most 64 MiB of HBM per device.

v0:
```python
import math
import jax
import jax.numpy as jnp
from jax import lax
from jax.sharding import PartitionSpec as P

HEAD = 128
BLOCK = 128
NEG_FILL = -1e30


def local(tokens_in, w_qkv, w_out, grad_y, block_cols, block_count):
    tok_rows = tokens_in.shape[0]
    heads_dev = w_out.shape[0] // HEAD
    local_blocks = tok_rows // BLOCK
    block_total = block_cols.shape[0]
    slot_total = block_cols.shape[1]
    score_scale = 1.0 / math.sqrt(HEAD)
    projected = jnp.einsum(
        "td,cde->cte", tokens_in, w_qkv, preferred_element_type=jnp.float32
    ).astype(jnp.bfloat16)
    heads_view = projected.reshape(3, tok_rows, heads_dev, HEAD)
    queries, keys_loc, values_loc = (heads_view[0], heads_view[1], heads_view[2])
    keys_all, values_all = (
        lax.all_gather(keys_loc, "blk", axis=0, tiled=True),
        lax.all_gather(values_loc, "blk", axis=0, tiled=True),
    )
    key_blocks = keys_all.reshape(block_total, BLOCK, heads_dev, HEAD)
    value_blocks = values_all.reshape(block_total, BLOCK, heads_dev, HEAD)
    row_ids = lax.axis_index("blk") * local_blocks + jnp.arange(local_blocks, dtype=jnp.int32)
    my_cols = jnp.take(block_cols, row_ids, axis=0)
    my_counts = jnp.take(block_count, row_ids, axis=0)
    q_blocks = queries.reshape(local_blocks, BLOCK, heads_dev, HEAD)

    def slot_operands(slot):
        col_ids = lax.dynamic_index_in_dim(my_cols, slot, 1, keepdims=False)
        live_rows = slot < my_counts
        k_part = jnp.take(key_blocks, col_ids, axis=0)
        v_part = jnp.take(value_blocks, col_ids, axis=0)
        raw_scores = (
            jnp.einsum("bqhe,bkhe->bhqk", q_blocks, k_part, preferred_element_type=jnp.float32)
            * score_scale
        )
        return (col_ids, live_rows, k_part, v_part, raw_scores)

    def stats_slot(slot, carried):
        run_max, run_sum = carried
        col_ids, live_rows, k_part, v_part, raw_scores = slot_operands(slot)
        live_wide = live_rows[:, None, None, None]
        masked = jnp.where(live_wide, raw_scores, NEG_FILL)
        new_max = jnp.maximum(run_max, jnp.max(masked, axis=3))
        exps = jnp.where(live_wide, jnp.exp(masked - new_max[..., None]), 0.0)
        run_sum = run_sum * jnp.exp(run_max - new_max) + jnp.sum(exps, axis=3)
        return (new_max, run_sum)

    start_max = jnp.full((local_blocks, heads_dev, BLOCK), NEG_FILL, jnp.float32)
    start_sum = jnp.zeros((local_blocks, heads_dev, BLOCK), jnp.float32)
    run_max, run_sum = lax.fori_loop(0, slot_total, stats_slot, (start_max, start_sum))
    log_sum = run_max + jnp.log(run_sum)

    def value_slot(slot, accumulated):
        col_ids, live_rows, k_part, v_part, raw_scores = slot_operands(slot)
        live_wide = live_rows[:, None, None, None]
        weights = jnp.where(live_wide, jnp.exp(raw_scores - log_sum[..., None]), 0.0).astype(
            jnp.bfloat16
        )
        return accumulated + jnp.einsum(
            "bhqk,bkhe->bhqe", weights, v_part, preferred_element_type=jnp.float32
        )

    start_acc = jnp.zeros((local_blocks, heads_dev, BLOCK, HEAD), jnp.float32)
    accumulated = lax.fori_loop(0, slot_total, value_slot, start_acc)
    attended_blk = accumulated.astype(jnp.bfloat16)
    attended = attended_blk.transpose(0, 2, 1, 3).reshape(tok_rows, heads_dev, HEAD)
    o_flat = attended.reshape(tok_rows, heads_dev * HEAD)
    grad_heads = (
        jnp.dot(grad_y, w_out.T, preferred_element_type=jnp.float32)
        .astype(jnp.bfloat16)
        .reshape(tok_rows, heads_dev, HEAD)
    )
    g_blocks = grad_heads.reshape(local_blocks, BLOCK, heads_dev, HEAD)
    delta_blk = jnp.einsum(
        "bhqe,bqhe->bhq", attended_blk.astype(jnp.float32), g_blocks.astype(jnp.float32)
    )
    block_range = jnp.arange(block_total, dtype=jnp.int32)

    def backward_slot(slot, carried):
        col_ids, live_rows, k_part, v_part, raw_scores = slot_operands(slot)
        live_wide = live_rows[:, None, None, None]
        prob_rows = jnp.where(live_wide, jnp.exp(raw_scores - log_sum[..., None]), 0.0)
        dprobs = jnp.einsum("bqhe,bkhe->bhqk", g_blocks, v_part, preferred_element_type=jnp.float32)
        dscores = (prob_rows * (dprobs - delta_blk[..., None])).astype(jnp.bfloat16)
        dq_acc = carried[0] + jnp.einsum(
            "bhqk,bkhe->bqhe", dscores, k_part, preferred_element_type=jnp.float32
        )
        owner = ((col_ids[:, None] == block_range[None, :]) & live_rows[:, None]).astype(
            jnp.float32
        )
        dk_term = (
            jnp.einsum("bhqk,bqhe->bkhe", dscores, q_blocks, preferred_element_type=jnp.float32)
            * score_scale
        )
        dv_term = jnp.einsum(
            "bhqk,bqhe->bkhe",
            prob_rows.astype(jnp.bfloat16),
            g_blocks,
            preferred_element_type=jnp.float32,
        )
        dk_full = carried[1] + jnp.einsum(
            "bn,bkhe->nkhe", owner, dk_term, precision=lax.Precision.HIGHEST
        )
        dv_full = carried[2] + jnp.einsum(
            "bn,bkhe->nkhe", owner, dv_term, precision=lax.Precision.HIGHEST
        )
        return (dq_acc, dk_full, dv_full)

    dq_start = jnp.zeros((local_blocks, BLOCK, heads_dev, HEAD), jnp.float32)
    full_zero = jnp.zeros((block_total, BLOCK, heads_dev, HEAD), jnp.float32)
    back_start = (dq_start, full_zero, full_zero)
    back_out = lax.fori_loop(0, slot_total, backward_slot, back_start)
    grad_q = (back_out[0] * score_scale).astype(jnp.bfloat16).reshape(tok_rows, heads_dev, HEAD)
    stacked = jnp.stack(
        [
            back_out[1].reshape(block_total * BLOCK, heads_dev, HEAD),
            back_out[2].reshape(block_total * BLOCK, heads_dev, HEAD),
        ],
        axis=1,
    )
    key_grads = lax.psum_scatter(stacked, "blk", scatter_dimension=0, tiled=True)
    grad_k = key_grads[:, 0].astype(jnp.bfloat16)
    grad_v = key_grads[:, 1].astype(jnp.bfloat16)
    grads_stack = jnp.stack([grad_q, grad_k, grad_v]).reshape(3, tok_rows, heads_dev * HEAD)
    dx_term = jnp.einsum("cte,cde->td", grads_stack, w_qkv, preferred_element_type=jnp.float32)
    grad_x = lax.psum_scatter(dx_term, "mp", scatter_dimension=1, tiled=True).astype(jnp.bfloat16)
    qkv_term = jnp.einsum("td,cte->cde", tokens_in, grads_stack, preferred_element_type=jnp.float32)
    out_term = jnp.dot(o_flat.T, grad_y, preferred_element_type=jnp.float32)
    grad_qkv, grad_out = (
        lax.psum_scatter(qkv_term, "blk", scatter_dimension=1, tiled=True),
        lax.psum_scatter(out_term, "blk", scatter_dimension=1, tiled=True),
    )
    return (grad_x, grad_qkv.astype(jnp.bfloat16), grad_out.astype(jnp.bfloat16))


def solution(mesh):
    in_specs = (P("blk", None), P(None, None, "mp"), P("mp", None), P("blk", None), P(), P())
    out_specs = (P("blk", "mp"), P(None, "blk", "mp"), P("mp", "blk"))
    return jax.shard_map(local, mesh=mesh, in_specs=in_specs, out_specs=out_specs, check_vma=False)
```

profile of v0, /device:TPU:0, one launch (start us, length us, event | category | flops | bytes accessed | tf_op | source)
XLA Modules:
  0.0 675.0 jit_solution(446797628690224736)
XLA Ops:
  7.2 5.0 fusion.40
  12.3 0.8 fusion.48
  13.2 0.7 all-gather.5.cloned.1.call-update
  15.2 0.6 gather_fusion.6
  16.0 2.0 convolution_convert_fusion.1
  18.1 49.0 %all-gather.3.cloned.1.call-done = bf16[2048,4,128]{0,2,1:T(8,128)(2,1)} async-done(((bf16[256,4,128]{0,2,1:T(8,128)(2,1)}), bf16[2048,4,128]{0,2,1:T(8,128)(2,1)}) %all-gather.3.cloned.1.call-update) | async-done | bytes 2097168 | tf_op jit(solution)/shard_map/all_gather | solution.py:25
  67.1 4.3 copy.39
  71.4 6.3 while.48
  71.4 2.4 gather_fusion
  74.6 2.5 gather_fusion
  77.7 41.2 %all-gather.5.cloned.1.call-done = bf16[2048,4,128]{0,2,1:T(8,128)(2,1)} async-done(((bf16[256,4,128]{0,2,1:T(8,128)(2,1)}), bf16[2048,4,128]{0,2,1:T(8,128)(2,1)}) %all-gather.5.cloned.1.call-update) | async-done | bytes 2097168 | tf_op jit(solution)/shard_map/all_gather | solution.py:26
  119.0 4.3 copy.42
  123.3 11.2 %while.49 = (s32[]{:T(128)}, f32[2,4,128,128]{3,2,1,0:T(8,128)S(1)}, s32[2]{0:T(128)S(1)}, s32[2,2]{0,1:T(2,128)S(1)}, bf16[16,128,4,128]{3,2,1,0:T(4,128)(2,1)}...) while((s32[]{:T(128)}, ...), condition=%wide.region_5.7_spmd.clone, body=%wide.region_4.6_spmd.clone.sunk | while | flops 68158480 | bytes 3941551 | solution.py:72
  123.3 2.4 gather_fusion.2
  125.7 2.4 gather_fusion.1
  128.9 2.4 gather_fusion.2
  131.3 2.4 gather_fusion.1
  134.5 0.8 copy-done.11
  135.3 1.1 convert_bitcast_fusion
  137.0 33.5 %while.50 = (s32[]{:T(128)}, f32[2,128,4,128]{1,3,2,0:T(8,128)S(1)}, f32[16,128,4,128]{3,0,2,1:T(8,128)}, f32[16,128,4,128]{3,0,2,1:T(8,128)}, s32[2,2]{0,1:T(2,...) while((s32[]{:T(128)}, ...), condition=%wide.region_7.9_spmd.clone, body=%wide.region_6.8_spmd.clone.sunk | while | flops 223872144 | bytes 93861216 | solution.py:120
  137.2 2.4 gather_fusion.4
  139.6 2.4 gather_fusion.3
  143.8 0.8 copy-done.5
  144.6 3.6 select_add_fusion.4
  148.2 3.6 select_add_fusion.5
  151.8 2.0 copy-done.4
  153.8 2.4 gather_fusion.4
  156.2 2.4 gather_fusion.3
  160.5 0.8 copy-done.5
  161.3 3.6 select_add_fusion.4
  164.9 3.6 select_add_fusion.5
  168.5 2.0 copy-done.4
  170.4 4.8 copy.50
  175.2 2.4 copy.49
  177.7 3.8 pad_maximum_fusion
  181.7 0.9 copy-done.9
  182.7 2.7 fusion.43
  185.8 143.0 %reduce-scatter.5.cloned.1.call-done = f32[256,2,4,128]{3,0,2,1:T(8,128)} async-done(((f32[2048,2,4,128]{3,0,2,1:T(8,128)}), f32[256,2,4,128]{3,0,2,1:T(8,128)}) %reduce-scatter.5.cloned.1.call-update) | async-done | bytes 1048592 | tf_op jit(solution)/shard_map/reduce_scatter | solution.py:129
  328.8 1.3 convert.7
  330.9 6.0 convolution_bitcast_fusion.2
  337.0 6.4 convolution_bitcast_fusion.1
  343.4 76.8 %reduce-scatter.11.cloned.1.call-done = f32[512,256]{1,0:T(8,128)} async-done(((f32[512,2048]{1,0:T(8,128)}), f32[512,256]{1,0:T(8,128)}) %reduce-scatter.11.cloned.1.call-update) | async-done | bytes 524304 | tf_op jit(solution)/shard_map/reduce_scatter | solution.py:139
  420.3 1.8 convert_element_type.81
  422.0 31.9 %reduce-scatter.7.cloned.1.call-done = f32[256,512]{1,0:T(8,128)} async-done(((f32[256,2048]{1,0:T(8,128)}), f32[256,512]{1,0:T(8,128)}) %reduce-scatter.7.cloned.1.call-update) | async-done | bytes 524304 | tf_op jit(solution)/shard_map/reduce_scatter | solution.py:134
  453.9 1.8 convert_element_type.79
  455.7 209.9 %reduce-scatter.9.cloned.1.call-done = f32[3,256,512]{1,2,0:T(8,128)} async-done(((f32[3,2048,512]{1,2,0:T(8,128)}), f32[3,256,512]{1,2,0:T(8,128)}) %reduce-scatter.9.cloned.1.call-update) | async-done | bytes 1572880 | tf_op jit(solution)/shard_map/reduce_scatter | solution.py:138
  665.5 1.5 convert_element_type.80
  667.0 1.2 copy.55
  (117 shorter events, 10.3 us)
Async XLA Ops:
  7.2 8.8 %copy-start = (bf16[512,2048]{1,0:T(8,128)(2,1)S(1)}, bf16[512,2048]{1,0:T(8,128)(2,1)}, u32[]{:S(2)}) copy-start(bf16[512,2048]{1,0:T(8,128)(2,1)} %param.16) | copy-start | bytes 6291460
  7.2 6.8 %copy-start.12 = (s32[16,2]{0,1:T(2,128)S(1)}, s32[16,2]{0,1:T(2,128)}, u32[]{:S(2)}) copy-start(s32[16,2]{0,1:T(2,128)} %param.18) | copy-start | bytes 388
  7.2 8.0 %copy-start.2 = (s32[16]{0:T(128)S(1)}, s32[16]{0:T(128)}, u32[]{:S(2)}) copy-start(s32[16]{0:T(128)} %param.19) | copy-start | bytes 196
  7.2 59.9 %all-gather.3.cloned.1.call-start = ((), (), s32[]{:S(2)}) async-start(), calls=%async_computation.4 | async-start | bytes 2359296 | tf_op jit(solution)/shard_map/all_gather | solution.py:25
  13.1 105.8 %all-gather.5.cloned.1.call-start = ((), (), s32[]{:S(2)}) async-start(), calls=%async_computation.5 | async-start | bytes 2359296 | tf_op jit(solution)/shard_map/all_gather | solution.py:26
  13.9 314.9 %reduce-scatter.5.cloned.1.call-start = ((), (), s32[]{:S(2)}) async-start(), calls=%async_computation.6 | async-start | bytes 9437184 | tf_op jit(solution)/shard_map/reduce_scatter | solution.py:129
  77.7 45.6 %copy-start.10 = (f32[2,4,128,128]{3,2,1,0:T(8,128)S(1)}, f32[2,4,128,128]{3,2,1,0:T(8,128)}, u32[]{:S(2)}) copy-start(f32[2,4,128,128]{3,2,1,0:T(8,128)} %custom-call.2) | copy-start | bytes 1572868
  134.5 0.8 copy-start.11
  142.4 2.2 copy-start.5
  144.6 3.6 copy-start.3
  148.2 3.6 copy-start.6
  151.8 2.0 copy-start.4
  159.1 2.2 copy-start.5
  161.3 3.6 copy-start.3
  164.9 3.6 copy-start.6
  168.4 2.0 copy-start.4
  170.4 4.8 copy-start.7
  181.5 1.2 copy-start.9
  181.5 238.8 %reduce-scatter.11.cloned.1.call-start = ((), (), s32[]{:S(2)}) async-start(), calls=%async_computation.9 | async-start | bytes 4718592 | tf_op jit(solution)/shard_map/reduce_scatter | solution.py:139
  185.4 268.5 %reduce-scatter.7.cloned.1.call-start = ((), (), s32[]{:S(2)}) async-start(), calls=%async_computation.7 | async-start | bytes 2621440 | tf_op jit(solution)/shard_map/reduce_scatter | solution.py:134
  330.9 6.1 copy-start.8
  337.0 328.6 %reduce-scatter.9.cloned.1.call-start = ((), (), s32[]{:S(2)}) async-start(), calls=%async_computation.8 | async-start | bytes 14155776 | tf_op jit(solution)/shard_map/reduce_scatter | solution.py:138
  343.4 324.8 %copy-start.1 = (bf16[512,2048]{1,0:T(8,128)(2,1)S(1)}, bf16[512,2048]{1,0:T(8,128)(2,1)}, u32[]{:S(2)}) copy-start(bf16[512,2048]{1,0:T(8,128)(2,1)} %param.16) | copy-start | bytes 6291460
Sparse Core Ops, SparseCore 0:
  13.3 53.7 all-gather.2
  69.7 49.2 all-gather.4
  181.6 147.1 reduce-scatter.4
  332.8 87.4 reduce-scatter.10
  422.6 31.2 reduce-scatter.6
  457.8 207.7 reduce-scatter.8
where the time goes:
time: 676 us; the launch traced here: 675 us
  waiting for transfers between devices  553 us (82%)
  local copies, waits for them, and re-layouts  52.7 us (8%)
  matrix products  40.6 us (6%)
  between operations  14.4 us (2%)
  other arithmetic  13.8 us (2%)
    reduce_scatter x1, waiting for transfers between devices, local(): lax.psum_scatter(qkv_term, 'blk', scatter_dimension=1, tiled=True)  210 us
    reduce_scatter x1, waiting for transfers between devices, local(): lax.psum_scatter(stacked, 'blk', scatter_dimension=0, tiled=True)  143 us
    reduce_scatter x1, waiting for transfers between devices, local(): lax.psum_scatter(out_term, 'blk', scatter_dimension=1, tiled=True)  76.8 us
    all_gather x1, waiting for transfers between devices, local(): lax.all_gather(keys_loc, 'blk', axis=0, tiled=True)  49 us
    all_gather x1, waiting for transfers between devices, local(): lax.all_gather(values_loc, 'blk', axis=0, tiled=True)  41.2 us
    reduce_scatter x1, waiting for transfers between devices, local(): lax.psum_scatter(dx_term, 'mp', scatter_dimension=1, tiled=True)  31.9 us
    gather x6, local copies, waits for them, and re-layouts, slot_operands(): k_part = jnp.take(key_blocks, col_ids, axis=0)  14.3 us
  transfers between devices with their start and end apart: 6, of which 6 were waited for; matrix products, arithmetic and copies ran while one was open for 5% of the time, Pallas kernels for 0%

commit v1 on v0

--- a/solution.py
+++ b/solution.py
@@ -7,6 +7,18 @@
 HEAD = 128
 BLOCK = 128
 NEG_FILL = -1e30
+
+
+def doubled_up(x, axis, dim):
+    ways, here = (lax.axis_size(axis), lax.axis_index(axis))
+    grown, reach = (x, 1)
+    while reach < ways:
+        theirs = lax.ppermute(grown, axis, [(d, d ^ reach) for d in range(ways)])
+        mine_first = jnp.concatenate([grown, theirs], axis=dim)
+        theirs_first = jnp.concatenate([theirs, grown], axis=dim)
+        grown = jnp.where(here & reach == 0, mine_first, theirs_first)
+        reach = 2 * reach
+    return grown
 
 
 def local(tokens_in, w_qkv, w_out, grad_y, block_cols, block_count):
@@ -23,7 +35,7 @@
     queries, keys_loc, values_loc = (heads_view[0], heads_view[1], heads_view[2])
     keys_all, values_all = (
         lax.all_gather(keys_loc, "blk", axis=0, tiled=True),
-        lax.all_gather(values_loc, "blk", axis=0, tiled=True),
+        doubled_up(values_loc, "blk", 0),
     )
     key_blocks = keys_all.reshape(block_total, BLOCK, heads_dev, HEAD)
     value_blocks = values_all.reshape(block_total, BLOCK, heads_dev, HEAD)

time: 676 us -> 687 us (1.016)
  other arithmetic: 13.8 us -> 22.4 us
  starting transfers between devices: 0.24 us -> 7.55 us
    ppermute x0 -> x3, waiting for transfers between devices: none -> 83.9 us  [doubled_up(): theirs = lax.ppermute(grown, axis, [(d, d ^ reach) for d in range(ways)])]
    all_gather x1, waiting for transfers between devices: 49 us -> 0.01 us  [local(): lax.all_gather(keys_loc, 'blk', axis=0, tiled=True)]
    all_gather x1 -> x0, waiting for transfers between devices: 41.2 us -> none  [local(): lax.all_gather(values_loc, 'blk', axis=0, tiled=True)]
    select_n x0 -> x3, other arithmetic: none -> 8.52 us  [doubled_up(): grown = jnp.where(here & reach == 0, mine_first, theirs_first)]
    ppermute x0 -> x3, starting transfers between devices: none -> 7.35 us  [doubled_up(): theirs = lax.ppermute(grown, axis, [(d, d ^ reach) for d in range(ways)])]
  transfers between devices with their start and end apart: 6 -> 8, of which waited for: 6 -> 7; matrix products, arithmetic and copies ran while one was open for 5% -> 6% of each run, Pallas kernels for 0% -> 0%
where the time goes in v1:
time: 687 us; the launch traced here: 686 us
  waiting for transfers between devices  548 us (80%)
  local copies, waits for them, and re-layouts  52.6 us (8%)
  matrix products  40.6 us (6%)
  other arithmetic  22.4 us (3%)
  between operations  14.1 us (2%)
  starting transfers between devices  7.55 us (1%)
    reduce_scatter x1, waiting for transfers between devices, local(): lax.psum_scatter(qkv_term, 'blk', scatter_dimension=1, tiled=True)  210 us
    reduce_scatter x1, waiting for transfers between devices, local(): lax.psum_scatter(stacked, 'blk', scatter_dimension=0, tiled=True)  146 us
    ppermute x3, waiting for transfers between devices, doubled_up(): theirs = lax.ppermute(grown, axis, [(d, d ^ reach) for d in range(ways)])  83.9 us
    reduce_scatter x1, waiting for transfers between devices, local(): lax.psum_scatter(out_term, 'blk', scatter_dimension=1, tiled=True)  77 us
    reduce_scatter x1, waiting for transfers between devices, local(): lax.psum_scatter(dx_term, 'mp', scatter_dimension=1, tiled=True)  31.8 us
    gather x6, local copies, waits for them, and re-layouts, slot_operands(): k_part = jnp.take(key_blocks, col_ids, axis=0)  14.3 us
  transfers between devices with their start and end apart: 8, of which 7 were waited for; matrix products, arithmetic and copies ran while one was open for 6% of the time, Pallas kernels for 0%

profile of v1, /device:TPU:0, one launch (start us, length us, event | category | flops | bytes accessed | tf_op | source)
XLA Modules:
  0.0 686.2 jit_solution(13511253557558873381)
XLA Ops:
  7.2 5.0 fusion.40
  13.1 3.0 collective-permute-start
  16.1 6.3 collective-permute-done
  23.4 1.8 collective-permute-start.1
  25.8 19.4 %collective-permute-done.1 = bf16[512,4,128]{0,2,1:T(8,128)(2,1)} collective-permute-done((bf16[512,4,128]{0,2,1:T(8,128)(2,1)}, bf16[512,4,128]{0,2,1:T(8,128)(2,1)}, u32[]{:S(2)}, u32[]{:S(2)}) %collective-permute-start.1) | collective-permute-done | bytes 524320 | tf_op jit(solution)/shard_map/ppermute | solution.py:16
  45.2 3.0 maximum_select_fusion.1
  48.2 2.5 collective-permute-start.2
  52.1 2.0 convolution_convert_fusion.1
  54.2 58.2 %collective-permute-done.2 = bf16[1024,4,128]{0,2,1:T(8,128)(2,1)} collective-permute-done((bf16[1024,4,128]{0,2,1:T(8,128)(2,1)}, bf16[1024,4,128]{0,2,1:T(8,128)(2,1)}, u32[]{:S(2)}, u32[]{:S(2)}) %collective-permute-start.2) | collective-permute-done | bytes 1048608 | tf_op jit(solution)/shard_map/ppermute | solution.py:16
  112.4 4.6 maximum_select_fusion
  117.0 4.3 copy.42
  121.3 4.3 copy.39
  125.6 6.3 while.48
  125.6 2.4 gather_fusion
  128.8 2.4 gather_fusion
  131.9 11.2 %while.49 = (s32[]{:T(128)}, f32[2,4,128,128]{3,2,1,0:T(8,128)S(1)}, s32[2]{0:T(128)S(1)}, s32[2,2]{0,1:T(2,128)S(1)}, bf16[16,128,4,128]{3,2,1,0:T(4,128)(2,1)}...) while((s32[]{:T(128)}, ...), condition=%wide.region_5.7_spmd.clone, body=%wide.region_4.6_spmd.clone.sunk | while | flops 68158480 | bytes 3941551 | solution.py:84
  131.9 2.4 gather_fusion.2
  134.3 2.4 gather_fusion.1
  137.6 2.4 gather_fusion.2
  140.0 2.4 gather_fusion.1
  143.9 1.1 convert_bitcast_fusion
  145.6 33.5 %while.50 = (s32[]{:T(128)}, f32[2,128,4,128]{1,3,2,0:T(8,128)S(1)}, f32[16,128,4,128]{3,0,2,1:T(8,128)}, f32[16,128,4,128]{3,0,2,1:T(8,128)}, s32[2,2]{0,1:T(2,...) while((s32[]{:T(128)}, ...), condition=%wide.region_7.9_spmd.clone, body=%wide.region_6.8_spmd.clone.sunk | while | flops 223872144 | bytes 93861216 | solution.py:132
  145.8 2.4 gather_fusion.4
  148.2 2.4 gather_fusion.3
  153.3 3.6 select_add_fusion.4
  156.9 3.6 select_add_fusion.5
  160.4 2.0 copy-done.4
  162.5 2.4 gather_fusion.4
  164.9 2.4 gather_fusion.3
  169.9 3.6 select_add_fusion.4
  173.5 3.6 select_add_fusion.5
  177.1 2.0 copy-done.4
  179.1 4.8 copy.50
  183.9 2.4 copy.49
  186.3 3.8 pad_maximum_fusion
  190.4 0.9 copy-done.9
  191.3 2.7 fusion.43
  194.5 145.7 %reduce-scatter.5.cloned.1.call-done = f32[256,2,4,128]{3,0,2,1:T(8,128)} async-done(((f32[2048,2,4,128]{3,0,2,1:T(8,128)}), f32[256,2,4,128]{3,0,2,1:T(8,128)}) %reduce-scatter.5.cloned.1.call-update) | async-done | bytes 1048592 | tf_op jit(solution)/shard_map/reduce_scatter | solution.py:141
  340.2 1.3 convert.7
  342.3 6.0 convolution_bitcast_fusion.2
  348.4 6.4 convolution_bitcast_fusion.1
  354.8 77.0 %reduce-scatter.11.cloned.1.call-done = f32[512,256]{1,0:T(8,128)} async-done(((f32[512,2048]{1,0:T(8,128)}), f32[512,256]{1,0:T(8,128)}) %reduce-scatter.11.cloned.1.call-update) | async-done | bytes 524304 | tf_op jit(solution)/shard_map/reduce_scatter | solution.py:151
  431.7 1.8 convert_element_type.81
  433.5 31.8 %reduce-scatter.7.cloned.1.call-done = f32[256,512]{1,0:T(8,128)} async-done(((f32[256,2048]{1,0:T(8,128)}), f32[256,512]{1,0:T(8,128)}) %reduce-scatter.7.cloned.1.call-update) | async-done | bytes 524304 | tf_op jit(solution)/shard_map/reduce_scatter | solution.py:146
  465.3 1.8 convert_element_type.79
  467.1 209.9 %reduce-scatter.9.cloned.1.call-done = f32[3,256,512]{1,2,0:T(8,128)} async-done(((f32[3,2048,512]{1,2,0:T(8,128)}), f32[3,256,512]{1,2,0:T(8,128)}) %reduce-scatter.9.cloned.1.call-update) | async-done | bytes 1572880 | tf_op jit(solution)/shard_map/reduce_scatter | solution.py:150
  677.0 1.5 convert_element_type.80
  678.5 1.2 copy.55
  (123 shorter events, 15.0 us)
Async XLA Ops:
  7.2 44.9 %copy-start = (bf16[512,2048]{1,0:T(8,128)(2,1)S(1)}, bf16[512,2048]{1,0:T(8,128)(2,1)}, u32[]{:S(2)}) copy-start(bf16[512,2048]{1,0:T(8,128)(2,1)} %param.16) | copy-start | bytes 6291460
  7.2 114.1 %all-gather.2.cloned.1.call-start = ((), (), s32[]{:S(2)}) async-start(), calls=%async_computation.4 | async-start | bytes 2359296 | tf_op jit(solution)/shard_map/all_gather | solution.py:37
  12.3 13.5 %copy-start.12 = (s32[16,2]{0,1:T(2,128)S(1)}, s32[16,2]{0,1:T(2,128)}, u32[]{:S(2)}) copy-start(s32[16,2]{0,1:T(2,128)} %param.18) | copy-start | bytes 388
  12.3 38.4 %copy-start.2 = (s32[16]{0:T(128)S(1)}, s32[16]{0:T(128)}, u32[]{:S(2)}) copy-start(s32[16]{0:T(128)} %param.19) | copy-start | bytes 196
  13.1 327.1 %reduce-scatter.5.cloned.1.call-start = ((), (), s32[]{:S(2)}) async-start(), calls=%async_computation.5 | async-start | bytes 9437184 | tf_op jit(solution)/shard_map/reduce_scatter | solution.py:141
  13.1 9.3 %collective-permute-start = (bf16[256,4,128]{0,2,1:T(8,128)(2,1)S(1)}, bf16[256,4,128]{0,2,1:T(8,128)(2,1)S(1)}, u32[]{:S(2)}, u32[]{:S(2)}) collective-permute-start(bf16[256,4,128]{0,2,1:T(8,128)(2,1)S(1)} %bitcast.114), channel_id=1, source_target_pairs={{0,4},{4,0},{8,12},{12,8},{16,20},{20,16},{24,28},{28,24},{1,5},{5... | collective-permute-start | bytes 786440 | tf_op jit(solution)/shard_map/ppermute | solution.py:16
  23.4 21.9 %collective-permute-start.1 = (bf16[512,4,128]{0,2,1:T(8,128)(2,1)}, bf16[512,4,128]{0,2,1:T(8,128)(2,1)}, u32[]{:S(2)}, u32[]{:S(2)}) collective-permute-start(bf16[512,4,128]{0,2,1:T(8,128)(2,1)} %maximum_select_fusion.2), channel_id=1, source_target_pairs={{0,8},{4,12},{8,0},{12,4},{16,24},{20,28},{24,16},{28,20},{1,9},{5... | collective-permute-start | bytes 1572872 | tf_op jit(solution)/shard_map/ppermute | solution.py:16
  48.2 64.2 %collective-permute-start.2 = (bf16[1024,4,128]{0,2,1:T(8,128)(2,1)}, bf16[1024,4,128]{0,2,1:T(8,128)(2,1)}, u32[]{:S(2)}, u32[]{:S(2)}) collective-permute-start(bf16[1024,4,128]{0,2,1:T(8,128)(2,1)} %maximum_select_fusion.1), channel_id=1, source_target_pairs={{0,16},{4,20},{8,24},{12,28},{16,0},{20,4},{24,8},{28,12},{1,17},{... | collective-permute-start | bytes 3145736 | tf_op jit(solution)/shard_map/ppermute | solution.py:16
  125.6 6.3 copy-start.10
  143.2 0.8 copy-start.11
  151.1 2.2 copy-start.5
  153.3 3.6 copy-start.3
  156.9 3.6 copy-start.6
  160.4 2.0 copy-start.4
  167.7 2.2 copy-start.5
  169.9 3.6 copy-start.3
  173.5 3.6 copy-start.6
  177.1 2.0 copy-start.4
  179.1 4.8 copy-start.7
  190.1 1.2 copy-start.9
  190.1 241.6 %reduce-scatter.11.cloned.1.call-start = ((), (), s32[]{:S(2)}) async-start(), calls=%async_computation.8 | async-start | bytes 4718592 | tf_op jit(solution)/shard_map/reduce_scatter | solution.py:151
  194.0 271.3 %reduce-scatter.7.cloned.1.call-start = ((), (), s32[]{:S(2)}) async-start(), calls=%async_computation.6 | async-start | bytes 2621440 | tf_op jit(solution)/shard_map/reduce_scatter | solution.py:146
  342.3 6.1 copy-start.8
  348.3 328.7 %reduce-scatter.9.cloned.1.call-start = ((), (), s32[]{:S(2)}) async-start(), calls=%async_computation.7 | async-start | bytes 14155776 | tf_op jit(solution)/shard_map/reduce_scatter | solution.py:150
  354.8 324.9 %copy-start.1 = (bf16[512,2048]{1,0:T(8,128)(2,1)S(1)}, bf16[512,2048]{1,0:T(8,128)(2,1)}, u32[]{:S(2)}) copy-start(bf16[512,2048]{1,0:T(8,128)(2,1)} %param.16) | copy-start | bytes 6291460
Sparse Core Ops, SparseCore 0:
  13.2 87.1 all-gather.1
  190.3 149.8 reduce-scatter.4
  344.3 87.4 reduce-scatter.10
  434.1 31.1 reduce-scatter.6
  469.2 207.7 reduce-scatter.8
